TPU v7x, 256 devices: a whole 4x4x8 slice. The times are simulated.
256 devices in a mesh: req: 8 (over y, core), ep: 32 (over x, z).
Axes of the slice: x: 4, y: 4, z: 8, core: 2. Of those that a mesh axis runs over, the one named last changes fastest.
Arguments:
- queries: bfloat16 [2048, 64, 576], P(('req', 'ep')), may hold values from -7 to 7
- latent_cache: bfloat16 [256, 512, 576], P(('req', 'ep')), may hold values from -3 to 3
- new_latents: bfloat16 [2048, 576], P(('req', 'ep')), may hold values from -4 to 4
- parents: int32 [128, 16], replicated, may hold values from 0 to 14, as said below
- cache_len: int32 [128], replicated, may hold values from 128 to 1024
- tokens: bfloat16 [2048, 7168], P(('req', 'ep')), may hold values from -6 to 6
- route_ids: int32 [2048, 8], P(('req', 'ep')), may hold values from 0 to 31, all different within a row; in each aligned block of 8 rows (0 to 7, 8 to 15, ...) at most 3 rows name the same one
- route_scores: float32 [2048, 8], P(('req', 'ep')), may hold values from 0.05 to 1
- w_gate: bfloat16 [32, 7168, 2048], P('ep', None, 'req'), may hold values from -0.0625 to 0.0625
- w_up: bfloat16 [32, 7168, 2048], P('ep', None, 'req'), may hold values from -0.0625 to 0.0625
- w_down: bfloat16 [32, 2048, 7168], P('ep', 'req'), may hold values from -0.125 to 0.125
Outputs:
- attention_out: bfloat16 [2048, 64, 512], P(('req', 'ep'))
- moe_out: bfloat16 [2048, 7168], P(('req', 'ep'))
Inputs may be any that keep to these rules, and one draw needn't show every extreme that they name: `route_ids`: each row names 8 different experts. Among the 8 tokens of one device (aligned blocks of 8 rows) no expert is named by more than 3 tokens, a bound that some block reaches. parents[q, 0] = 0 and parents[q, j] < j for j >= 1.
All inputs are finite; a program needn't handle non-finite values.
Results may differ from a plain program's by a relative error of at most 0.015.
Values may be sent and summed in bfloat16 or wider, within the bound.
A program may use at most 128 MiB of HBM per device.

v0:
```python
import jax
import jax.numpy as jnp
from jax import lax
from jax.sharding import PartitionSpec as P

VDIM = 512
score_scale = 192.0 ** (-0.5)
route_scale = 2.5


def partner(block, axis, stride):
    count = lax.axis_size(axis)
    route = []
    for low in range(count):
        high = low | 1 << stride
        if high != low and high < count:
            route += [(low, high), (high, low)]
    return lax.ppermute(block, axis, route)


def ancestor_table(parent_row):
    node_count = parent_row.shape[0]
    node_ids = jnp.arange(node_count, dtype=jnp.int32)
    current = node_ids
    visible = node_ids[:, None] == node_ids[None, :]
    for repeat in range(node_count):
        current = parent_row[current]
        visible = visible | (current[:, None] == node_ids[None, :])
    return visible


def expert_mlp(row_block, w_gate, w_up, w_down):
    gate_val = jnp.dot(row_block, w_gate[0], preferred_element_type=jnp.float32)
    up_val = jnp.dot(row_block, w_up[0], preferred_element_type=jnp.float32)
    hidden = (jax.nn.silu(gate_val) * up_val).astype(jnp.bfloat16)
    return jnp.dot(hidden, w_down[0], preferred_element_type=jnp.float32).astype(jnp.bfloat16)


def body(
    queries,
    latent_cache,
    new_latents,
    parents,
    cache_len,
    tokens,
    route_ids,
    route_scores,
    w_gate,
    w_up,
    w_down,
):
    ep_count = lax.axis_size("ep")
    position = lax.axis_index("req") * ep_count + lax.axis_index("ep")
    request = position // 2
    half_index = position % 2
    tok_dev = tokens.shape[0]
    model_width = tokens.shape[1]
    other_cache, other_fresh = partner((latent_cache, new_latents), "ep", 0)
    lower_half = half_index == 0
    cache_rows = jnp.concatenate(
        [
            jnp.where(lower_half, latent_cache[0], other_cache[0]),
            jnp.where(lower_half, other_cache[0], latent_cache[0]),
        ],
        axis=0,
    )
    fresh_rows = jnp.concatenate(
        [
            jnp.where(lower_half, new_latents, other_fresh),
            jnp.where(lower_half, other_fresh, new_latents),
        ],
        axis=0,
    )
    key_rows = jnp.concatenate([cache_rows, fresh_rows], axis=0)
    context = cache_rows.shape[0]
    parent_row = lax.dynamic_index_in_dim(parents, request, 0, keepdims=False)
    tree_vis = lax.dynamic_slice_in_dim(
        ancestor_table(parent_row), half_index * tok_dev, tok_dev, 0
    )
    length = lax.dynamic_index_in_dim(cache_len, request, 0, keepdims=False)
    cached = jnp.arange(context, dtype=jnp.int32) < length
    visible = jnp.concatenate(
        [jnp.broadcast_to(cached[None, :], (tok_dev, context)), tree_vis], axis=1
    )
    head_count = queries.shape[1]
    flat_query = queries.reshape(tok_dev * head_count, queries.shape[2])
    scores = (
        lax.dot_general(
            flat_query, key_rows, (((1,), (1,)), ((), ())), preferred_element_type=jnp.float32
        )
        * score_scale
    )
    scores = scores.reshape(tok_dev, head_count, key_rows.shape[0])
    masked = jnp.where(visible[:, None, :], scores, -jnp.inf)
    row_max = jnp.max(masked, axis=-1, keepdims=True)
    shifted = jnp.exp(masked - row_max)
    attn_probs = (shifted / jnp.sum(shifted, axis=-1, keepdims=True)).astype(jnp.bfloat16)
    value_rows = key_rows[:, :VDIM]
    attended = jnp.dot(
        attn_probs.reshape(tok_dev * head_count, key_rows.shape[0]),
        value_rows,
        preferred_element_type=jnp.float32,
    )
    attention_out = attended.reshape(tok_dev, head_count, VDIM).astype(jnp.bfloat16)
    top_count = route_ids.shape[1]
    capacity = min(tok_dev, tok_dev * top_count // ep_count + 1)
    route_weight = route_scale * route_scores / jnp.sum(route_scores, axis=1, keepdims=True)
    pair_ids = route_ids.reshape(-1)
    onehot = (pair_ids[:, None] == jnp.arange(ep_count, dtype=jnp.int32)[None, :]).astype(jnp.int32)
    slot_rank = jnp.sum(jnp.cumsum(onehot, axis=0) * onehot, axis=1) - 1
    slot_of = (pair_ids * capacity + slot_rank).reshape(tok_dev, top_count)
    slot_ids = jnp.arange(ep_count * capacity, dtype=jnp.int32)
    slot_hits = slot_of[None, :, :] == slot_ids[:, None, None]
    dispatch = jnp.any(slot_hits, axis=2).astype(jnp.bfloat16)
    combine = jnp.sum(jnp.where(slot_hits, route_weight[None, :, :], 0.0), axis=2)
    outgoing = jnp.dot(dispatch, tokens, preferred_element_type=jnp.float32).astype(jnp.bfloat16)
    outgoing = outgoing.reshape(ep_count, capacity, model_width)
    arrived = lax.all_to_all(outgoing, "ep", split_axis=0, concat_axis=0, tiled=True)
    partial_value = expert_mlp(
        lax.all_gather(
            arrived.reshape(ep_count * capacity, model_width), "req", axis=0, tiled=True
        ),
        w_gate,
        w_up,
        w_down,
    )
    summed = lax.psum_scatter(
        partial_value.astype(jnp.float32).astype(jnp.bfloat16),
        "req",
        scatter_dimension=0,
        tiled=True,
    ).astype(jnp.float32)
    summed = summed.reshape(ep_count, capacity, model_width)
    returned = lax.all_to_all(
        summed.astype(jnp.bfloat16), "ep", split_axis=0, concat_axis=0, tiled=True
    ).astype(summed.dtype)
    moe_out = lax.dot_general(
        combine,
        returned.reshape(ep_count * capacity, model_width),
        (((0,), (0,)), ((), ())),
        precision=lax.Precision.HIGHEST,
        preferred_element_type=jnp.float32,
    )
    return (attention_out, moe_out.astype(jnp.bfloat16))


def solution(mesh):
    placed = (
        P(("req", "ep"), None, None),
        P(("req", "ep"), None, None),
        P(("req", "ep"), None),
        P(),
        P(),
        P(("req", "ep"), None),
        P(("req", "ep"), None),
        P(("req", "ep"), None),
        P("ep", None, "req"),
        P("ep", None, "req"),
        P("ep", "req", None),
    )
    return jax.shard_map(
        body,
        mesh=mesh,
        in_specs=placed,
        out_specs=(P(("req", "ep"), None, None), P(("req", "ep"), None)),
        check_vma=False,
    )
```

profile of v0, /device:TPU:32, one launch (start us, length us, event | category | flops | bytes accessed | tf_op | source)
XLA Modules:
  0.0 299.1 jit_solution(5161164357514581001)
XLA Ops:
  7.2 0.8 eq.306
  8.5 0.7 multiply_add_fusion
  9.3 2.5 convolution_convert_fusion.1
  11.8 2.6 reshape.271
  14.5 56.6 %all_to_all.10 = bf16[32,3,7168]{2,1,0:T(4,128)(2,1)} all-to-all(bf16[32,3,7168]{2,1,0:T(4,128)(2,1)S(1)} %reshape.271), channel_id=1, replica_groups=mesh['req'=8,'ep'=32] {'ep'}, dimensions={0} | all-to-all | bytes 2752512 | tf_op jit(solution)/shard_map/all_to_all | solution.py:118
  71.1 4.1 %reshape.272 = bf16[96,7168]{1,0:T(8,128)(2,1)} reshape(bf16[32,3,7168]{2,1,0:T(4,128)(2,1)} %all_to_all.10) | data formatting | bytes 2752512 | tf_op jit(solution)/shard_map/reshape | solution.py:121
  75.3 59.8 %all-gather.2.cloned.1.call-done = bf16[768,7168]{1,0:T(8,128)(2,1)} async-done(((bf16[96,7168]{1,0:T(8,128)(2,1)}), bf16[768,7168]{1,0:T(8,128)(2,1)}) %all-gather.2.cloned.1.call-update) | async-done | bytes 11010064 | tf_op jit(solution)/shard_map/all_gather | solution.py:120
  135.2 6.9 %fusion.3 = f32[768,256]{1,0:T(8,128)S(1)} fusion(bf16[768,7168]{1,0:T(8,128)(2,1)} %all-gather.2.cloned.1.call-done, bf16[1,7168,256]{2,1,0:T(8,128)(2,1)} %param.19), kind=kOutput, calls=%fused_computation.22 | convolution fusion | flops 2818572288 | bytes 15466496 | tf_op jit(solution)/shard_map/dot_general | solution.py:33
  142.0 18.9 %convolution_convert_fusion = bf16[768,7168]{1,0:T(8,128)(2,1)} fusion(bf16[1,256,7168]{2,1,0:T(8,128)(2,1)} %param.21, bf16[768,7168]{1,0:T(8,128)(2,1)} %all-gather.2.cloned.1.call-done, bf16[1,7168,256]{2,1,0:T(8,128)(2,1)} %param.20, f32[768,256]{1,0:T(8,128)S(1)} %fusion.3), kind=kOutput, calls=%fused_computation.16 | convolution fusion | flops 5643829248 | bytes 30146560 | tf_op jit(solution)/shard_map/dot_general | solution.py:36
  161.7 1.4 collective-permute-start.1
  176.1 52.9 %reduce-scatter.2.cloned.1.call-done = bf16[96,7168]{1,0:T(8,128)(2,1)} async-done(((bf16[768,7168]{1,0:T(8,128)(2,1)}), bf16[96,7168]{1,0:T(8,128)(2,1)}) %reduce-scatter.2.cloned.1.call-update) | async-done | bytes 1376272 | tf_op jit(solution)/shard_map/reduce_scatter | solution.py:127
  229.0 4.0 %convert_element_type.37 = bf16[32,3,7168]{2,1,0:T(4,128)(2,1)} reshape(bf16[96,7168]{1,0:T(8,128)(2,1)} %reduce-scatter.2.cloned.1.call-done) | data formatting | bytes 2752512 | tf_op jit(solution)/shard_map/convert_element_type | solution.py:135
  232.9 10.2 %all-to-all-start.1 = ((bf16[32,3,7168]{2,1,0:T(4,128)(2,1)}), bf16[32,3,7168]{2,1,0:T(4,128)(2,1)S(1)}, u32[]{:S(2)}, u32[]{:S(2)}) async-start(bf16[32,3,7168]{2,1,0:T(4,128)(2,1)} %convert_element_type.37), calls=%async_computation.2 | async-start | bytes 3670016 | tf_op jit(solution)/shard_map/all_to_all | solution.py:134
  244.0 1.4 copy.28
  245.4 1.0 broadcast_in_dim.21
  246.4 2.4 copy.32
  248.8 2.2 copy.29
  251.0 1.3 select_bitcast_fusion.1
  252.3 1.1 fusion.70
  254.2 1.4 copy.33
  255.6 3.2 %convolution_convert_fusion.3 = bf16[8,64,512]{2,1,0:T(8,128)(2,1)} fusion(bf16[8,64,1040]{2,1,0:T(8,128)(2,1)} %bitcast.100, bf16[8,576]{1,0:T(8,128)(2,1)} %copy-done.8, bf16[8,576]{1,0:T(8,128)(2,1)} %copy-done.7, bf16[512,576]{1,0:T(8,128)(2,1)} %copy-done.2, bf16[512,576]{1,0:T(8,128)(2,1)} %copy-done.1), kind=kOutput, calls=%fused_computation.37 | convolution fusion | flops 549781504 | bytes 2787328 | tf_op jit(solution)/shard_map/dot_general | solution.py:99
  258.8 28.4 %all-to-all-done.1 = bf16[32,3,7168]{2,1,0:T(4,128)(2,1)S(1)} async-done(((bf16[32,3,7168]{2,1,0:T(4,128)(2,1)}), bf16[32,3,7168]{2,1,0:T(4,128)(2,1)S(1)}, u32[]{:S(2)}, u32[]{:S(2)}) %all-to-all-start.1) | async-done | bytes 1376288 | tf_op jit(solution)/shard_map/all_to_all | solution.py:134
  287.2 2.4 reshape.273
  289.6 2.6 convolution_convert_fusion.2
  (101 shorter events, 15.7 us)
Async XLA Ops:
  7.2 245.1 %copy-start = (bf16[8,64,576]{2,1,0:T(8,128)(2,1)S(1)}, bf16[8,64,576]{2,1,0:T(8,128)(2,1)}, u32[]{:S(2)}) copy-start(bf16[8,64,576]{2,1,0:T(8,128)(2,1)} %param.11) | copy-start | bytes 1769476
  7.2 128.0 %all-gather.2.cloned.1.call-start = ((), (), s32[]{:S(2)}) async-start(), calls=%async_computation.3 | async-start | bytes 12386304 | tf_op jit(solution)/shard_map/all_gather | solution.py:120
  75.3 153.7 %reduce-scatter.2.cloned.1.call-start = ((), (), s32[]{:S(2)}) async-start(), calls=%async_computation.4 | async-start | bytes 12386304 | tf_op jit(solution)/shard_map/reduce_scatter | solution.py:127
  161.0 0.7 copy-start.6
  161.0 2.1 copy-start.9
  161.0 87.8 %collective-permute-start = (bf16[1,512,576]{1,2,0:T(8,128)(2,1)}, bf16[1,512,576]{1,2,0:T(8,128)(2,1)}, u32[]{:S(2)}, u32[]{:S(2)}) collective-permute-start(bf16[1,512,576]{1,2,0:T(8,128)(2,1)} %param.12), channel_id=1, source_target_pairs={{0,1},{1,0},{2,3},{3,2},{4,5},{5,4},{6,7},{7,6},{8,9},{9,8},{10,11... | collective-permute-start | bytes 1769480 | tf_op jit(solution)/shard_map/ppermute | solution.py:18
  161.7 87.1 %collective-permute-start.1 = (bf16[8,576]{1,0:T(8,128)(2,1)S(1)}, bf16[8,576]{1,0:T(8,128)(2,1)S(1)}, u32[]{:S(2)}, u32[]{:S(2)}) collective-permute-start(bf16[8,576]{1,0:T(8,128)(2,1)S(1)} %copy-done.6), channel_id=1, source_target_pairs={{0,1},{1,0},{2,3},{3,2},{4,5},{5,4},{6,7},{7,6},{8,9},{9,8},{10,11... | collective-permute-start | bytes 27656 | tf_op jit(solution)/shard_map/ppermute | solution.py:18
  168.8 5.8 %copy-start.10 = (s32[128]{0:T(128)S(1)}, s32[128]{0:T(128)}, u32[]{:S(2)}) copy-start(s32[128]{0:T(128)} %param.15) | copy-start | bytes 1540
  232.9 10.2 %copy-start.5 = (f32[8,8]{1,0:T(8,128)S(1)}, f32[8,8]{1,0:T(8,128)}, u32[]{:S(2)}) copy-start(f32[8,8]{1,0:T(8,128)} %param.18) | copy-start | bytes 772
  232.9 54.3 %all-to-all-start.1 = ((bf16[32,3,7168]{2,1,0:T(4,128)(2,1)}), bf16[32,3,7168]{2,1,0:T(4,128)(2,1)S(1)}, u32[]{:S(2)}, u32[]{:S(2)}) async-start(bf16[32,3,7168]{2,1,0:T(4,128)(2,1)} %convert_element_type.37), calls=%async_computation.2 | async-start | bytes 3670016 | tf_op jit(solution)/shard_map/all_to_all | solution.py:134
  248.8 4.7 %copy-start.7 = (bf16[8,576]{1,0:T(8,128)(2,1)}, bf16[8,576]{1,0:T(8,128)(2,1)S(1)}, u32[]{:S(2)}) copy-start(bf16[8,576]{1,0:T(8,128)(2,1)S(1)} %get-tuple-element.4) | copy-start | bytes 27652
  248.8 4.7 %copy-start.8 = (bf16[8,576]{1,0:T(8,128)(2,1)}, bf16[8,576]{1,0:T(8,128)(2,1)S(1)}, u32[]{:S(2)}) copy-start(bf16[8,576]{1,0:T(8,128)(2,1)S(1)} %get-tuple-element.5) | copy-start | bytes 27652
  251.0 1.3 copy-start.3
  252.3 1.2 copy-start.1
  252.3 1.2 copy-start.2
  258.8 30.7 %copy-start.4 = (f32[96,8]{0,1:T(8,128)S(1)}, f32[96,8]{0,1:T(8,128)}, u32[]{:S(2)}) copy-start(f32[96,8]{0,1:T(8,128)} %select_reduce_fusion) | copy-start | bytes 9220
Sparse Core Ops, SparseCore 0:
  75.4 59.7 all-gather.1
  161.1 67.8 reduce-scatter.1
where the time goes:
time: 300 us; the launch traced here: 299 us
  waiting for transfers between devices  141 us (47%)
  blocking collectives  56.6 us (19%)
  matrix products  35.4 us (12%)
  local copies, waits for them, and re-layouts  34.2 us (11%)
  between operations  14.4 us (5%)
  starting transfers between devices  12.2 us (4%)
  other arithmetic  5.09 us (2%)
    all_gather x1, waiting for transfers between devices, body(): lax.all_gather(arrived.reshape(ep_count * capacity, model_width), 'req',...  59.8 us
    all_to_all x1, blocking collectives, body(): lax.all_to_all(outgoing, 'ep', split_axis=0, concat_axis=0, tiled=True)  56.6 us
    reduce_scatter x1, waiting for transfers between devices, body(): lax.psum_scatter(partial_value.astype(jnp.float32).astype(jnp.bfloat16),...  52.9 us
    all_to_all x1, waiting for transfers between devices, body(): lax.all_to_all(summed.astype(jnp.bfloat16), 'ep', split_axis=0, concat_ax...  28.4 us
    dot_general x1, matrix products, expert_mlp(): jnp.dot(hidden, w_down[0], preferred_element_type=jnp.float32)  18.9 us
    gather x16, local copies, waits for them, and re-layouts, ancestor_table(): current = parent_row[current]  10.5 us
    all_to_all x1, starting transfers between devices, body(): lax.all_to_all(summed.astype(jnp.bfloat16), 'ep', split_axis=0, concat_ax...  10.2 us
    dot_general x1, matrix products, expert_mlp(): gate_val = jnp.dot(row_block, w_gate[0], preferred_element_type=jnp.float32)  6.88 us
  transfers between devices with their start and end apart: 5, of which 3 were waited for; matrix products, arithmetic and copies ran while one was open for 11% of the time, Pallas kernels for 0%

commit v1 on v0

--- a/solution.py
+++ b/solution.py
@@ -117,8 +117,16 @@
     outgoing = outgoing.reshape(ep_count, capacity, model_width)
     arrived = lax.all_to_all(outgoing, "ep", split_axis=0, concat_axis=0, tiled=True)
     partial_value = expert_mlp(
-        lax.all_gather(
-            arrived.reshape(ep_count * capacity, model_width), "req", axis=0, tiled=True
+        jnp.concatenate(
+            jax.lax.all_to_all(
+                jnp.stack(
+                    [arrived.reshape(ep_count * capacity, model_width)] * jax.lax.axis_size("req")
+                ),
+                "req",
+                0,
+                0,
+            ),
+            axis=0,
         ),
         w_gate,
         w_up,

time: 300 us -> 368 us (1.23)
  blocking collectives: 56.6 us -> 186 us
  waiting for transfers between devices: 141 us -> 74.8 us
  local copies, waits for them, and re-layouts: 34.2 us -> 43.1 us
  matrix products: 35.4 us -> 31.5 us
    all_to_all x0 -> x1, blocking collectives: none -> 129 us  [body(): jax.lax.all_to_all(jnp.stack([arrived.reshape(ep_count * capacity, model_...]
    all_gather x1 -> x0, waiting for transfers between devices: 59.8 us -> none  [body(): lax.all_gather(arrived.reshape(ep_count * capacity, model_width), 'req',...]
    another operation x0 -> x2, local copies, waits for them, and re-layouts: none -> 8.51 us  [body(): jnp.stack([arrived.reshape(ep_count * capacity, model_width)] * jax.lax.a...]
    reduce_scatter x1, waiting for transfers between devices: 52.9 us -> 46.4 us  [body(): lax.psum_scatter(partial_value.astype(jnp.float32).astype(jnp.bfloat16),...]
    unnamed x23 -> x27, local copies, waits for them, and re-layouts: 1.52 us -> 6.11 us
    reshape x1 -> x0, local copies, waits for them, and re-layouts: 4.14 us -> none  [body(): arrived.reshape(ep_count * capacity, model_width)]
    dot_general x1, matrix products: 6.88 us -> 3 us  [expert_mlp(): gate_val = jnp.dot(row_block, w_gate[0], preferred_element_type=jnp.float32)]
  transfers between devices with their start and end apart: 5 -> 4, of which waited for: 3 -> 2; matrix products, arithmetic and copies ran while one was open for 11% -> 9% of each run, Pallas kernels for 0% -> 0%
where the time goes in v1:
time: 368 us; the launch traced here: 367 us
  blocking collectives  186 us (51%)
  waiting for transfers between devices  74.8 us (20%)
  local copies, waits for them, and re-layouts  43.1 us (12%)
  matrix products  31.5 us (9%)
  between operations  14.4 us (4%)
  starting transfers between devices  12.2 us (3%)
  other arithmetic  5.1 us (1%)
    all_to_all x1, blocking collectives, body(): jax.lax.all_to_all(jnp.stack([arrived.reshape(ep_count * capacity, model_...  129 us
    all_to_all x1, blocking collectives, body(): lax.all_to_all(outgoing, 'ep', split_axis=0, concat_axis=0, tiled=True)  56.6 us
    reduce_scatter x1, waiting for transfers between devices, body(): lax.psum_scatter(partial_value.astype(jnp.float32).astype(jnp.bfloat16),...  46.4 us
    all_to_all x1, waiting for transfers between devices, body(): lax.all_to_all(summed.astype(jnp.bfloat16), 'ep', split_axis=0, concat_ax...  28.4 us
    dot_general x1, matrix products, expert_mlp(): jnp.dot(hidden, w_down[0], preferred_element_type=jnp.float32)  18.9 us
    gather x16, local copies, waits for them, and re-layouts, ancestor_table(): current = parent_row[current]  10.5 us
    all_to_all x1, starting transfers between devices, body(): lax.all_to_all(summed.astype(jnp.bfloat16), 'ep', split_axis=0, concat_ax...  10.2 us
    another operation x2, local copies, waits for them, and re-layouts, body(): jnp.stack([arrived.reshape(ep_count * capacity, model_width)] * jax.lax.a...  8.51 us
  transfers between devices with their start and end apart: 4, of which 2 were waited for; matrix products, arithmetic and copies ran while one was open for 9% of the time, Pallas kernels for 0%

profile of v1, /device:TPU:32, one launch (start us, length us, event | category | flops | bytes accessed | tf_op | source)
XLA Modules:
  0.0 366.9 jit_solution(14014648368198775701)
XLA Ops:
  9.3 2.5 convolution_convert_fusion.1
  11.8 2.6 reshape.273
  14.5 56.6 %all_to_all.15 = bf16[32,3,7168]{2,1,0:T(4,128)(2,1)} all-to-all(bf16[32,3,7168]{2,1,0:T(4,128)(2,1)S(1)} %reshape.273), channel_id=1, replica_groups=mesh['req'=8,'ep'=32] {'ep'}, dimensions={0} | all-to-all | bytes 2752512 | tf_op jit(solution)/shard_map/all_to_all | solution.py:118
  71.1 3.0 stack_reshape.2
  74.1 5.5 %stack.3 = bf16[8,96,7168]{2,1,0:T(8,128)(2,1)} broadcast(bf16[96,7168]{1,0:T(8,128)(2,1)S(1)} %stack_reshape.2), dimensions={1,2} | broadcast | bytes 12386304 | tf_op jit(solution)/shard_map/stack | solution.py:122
  79.6 129.2 %all_to_all.16 = bf16[8,96,7168]{2,1,0:T(8,128)(2,1)S(1)} all-to-all(bf16[8,96,7168]{2,1,0:T(8,128)(2,1)} %stack.3), channel_id=1, replica_groups=mesh['req'=8,'ep'=32] {'req'}, dimensions={0} | all-to-all | bytes 22020096 | tf_op jit(solution)/shard_map/all_to_all | solution.py:121
  208.8 4.0 %copy-done.1 = bf16[8,96,7168]{2,1,0:T(8,128)(2,1)} copy-done((bf16[8,96,7168]{2,1,0:T(8,128)(2,1)}, bf16[8,96,7168]{2,1,0:T(8,128)(2,1)S(1)}, u32[]{:S(2)}) %copy-start.1) | copy-done | bytes 11010072
  212.8 3.0 fusion.3
  215.8 18.9 %convolution_convert_fusion = bf16[768,7168]{1,0:T(8,128)(2,1)} fusion(bf16[1,256,7168]{2,1,0:T(8,128)(2,1)} %param.21, bf16[768,7168]{1,0:T(8,128)(2,1)} %bitcast.101, bf16[1,7168,256]{2,1,0:T(8,128)(2,1)} %param.20, f32[768,256]{1,0:T(8,128)S(1)} %fusion.3), kind=kOutput, calls=%fused_computation.16 | convolution fusion | flops 5643829248 | bytes 30146560 | tf_op jit(solution)/shard_map/dot_general | solution.py:36
  235.8 1.7 collective-permute-start
  250.4 46.4 %reduce-scatter.2.cloned.1.call-done = bf16[96,7168]{1,0:T(8,128)(2,1)} async-done(((bf16[768,7168]{1,0:T(8,128)(2,1)}), bf16[96,7168]{1,0:T(8,128)(2,1)}) %reduce-scatter.2.cloned.1.call-update) | async-done | bytes 1376272 | tf_op jit(solution)/shard_map/reduce_scatter | solution.py:135
  296.8 4.0 %convert_element_type.37 = bf16[32,3,7168]{2,1,0:T(4,128)(2,1)} reshape(bf16[96,7168]{1,0:T(8,128)(2,1)} %reduce-scatter.2.cloned.1.call-done) | data formatting | bytes 2752512 | tf_op jit(solution)/shard_map/convert_element_type | solution.py:143
  300.8 10.2 %all-to-all-start.2 = ((bf16[32,3,7168]{2,1,0:T(4,128)(2,1)}), bf16[32,3,7168]{2,1,0:T(4,128)(2,1)S(1)}, u32[]{:S(2)}, u32[]{:S(2)}) async-start(bf16[32,3,7168]{2,1,0:T(4,128)(2,1)} %convert_element_type.37), calls=%async_computation.3 | async-start | bytes 3670016 | tf_op jit(solution)/shard_map/all_to_all | solution.py:142
  311.9 1.4 copy.28
  313.2 1.0 broadcast_in_dim.21
  314.2 2.4 copy.32
  316.7 2.2 copy.29
  318.8 1.3 select_bitcast_fusion.1
  320.2 1.2 fusion.70
  322.1 1.4 copy.33
  323.5 3.2 convolution_convert_fusion.3
  326.7 28.4 %all-to-all-done.2 = bf16[32,3,7168]{2,1,0:T(4,128)(2,1)S(1)} async-done(((bf16[32,3,7168]{2,1,0:T(4,128)(2,1)}), bf16[32,3,7168]{2,1,0:T(4,128)(2,1)S(1)}, u32[]{:S(2)}, u32[]{:S(2)}) %all-to-all-start.2) | async-done | bytes 1376288 | tf_op jit(solution)/shard_map/all_to_all | solution.py:142
  355.1 2.4 reshape.275
  357.4 2.6 convolution_convert_fusion.2
  (104 shorter events, 17.5 us)
Async XLA Ops:
  7.2 313.0 %copy-start = (bf16[8,64,576]{2,1,0:T(8,128)(2,1)S(1)}, bf16[8,64,576]{2,1,0:T(8,128)(2,1)}, u32[]{:S(2)}) copy-start(bf16[8,64,576]{2,1,0:T(8,128)(2,1)} %param.11) | copy-start | bytes 1769476
  7.2 289.6 %reduce-scatter.2.cloned.1.call-start = ((), (), s32[]{:S(2)}) async-start(), calls=%async_computation.4 | async-start | bytes 12386304 | tf_op jit(solution)/shard_map/reduce_scatter | solution.py:135
  79.6 133.2 %copy-start.11 = (bf16[1,7168,256]{2,1,0:T(8,128)(2,1)S(1)}, bf16[1,7168,256]{2,1,0:T(8,128)(2,1)}, u32[]{:S(2)}) copy-start(bf16[1,7168,256]{2,1,0:T(8,128)(2,1)} %param.19) | copy-start | bytes 11010052
  208.8 4.0 %copy-start.1 = (bf16[8,96,7168]{2,1,0:T(8,128)(2,1)}, bf16[8,96,7168]{2,1,0:T(8,128)(2,1)S(1)}, u32[]{:S(2)}) copy-start(bf16[8,96,7168]{2,1,0:T(8,128)(2,1)S(1)} %all_to_all.16) | copy-start | bytes 33030148
  234.8 0.7 copy-start.7
  234.8 2.7 copy-start.12
  234.8 3.3 copy-start.10
  235.5 81.2 %collective-permute-start.1 = (bf16[8,576]{1,0:T(8,128)(2,1)S(1)}, bf16[8,576]{1,0:T(8,128)(2,1)S(1)}, u32[]{:S(2)}, u32[]{:S(2)}) collective-permute-start(bf16[8,576]{1,0:T(8,128)(2,1)S(1)} %copy-done.7), channel_id=1, source_target_pairs={{0,1},{1,0},{2,3},{3,2},{4,5},{5,4},{6,7},{7,6},{8,9},{9,8},{10,11... | collective-permute-start | bytes 27656 | tf_op jit(solution)/shard_map/ppermute | solution.py:18
  235.8 80.9 %collective-permute-start = (bf16[1,512,576]{1,2,0:T(8,128)(2,1)}, bf16[1,512,576]{1,2,0:T(8,128)(2,1)}, u32[]{:S(2)}, u32[]{:S(2)}) collective-permute-start(bf16[1,512,576]{1,2,0:T(8,128)(2,1)} %param.12), channel_id=1, source_target_pairs={{0,1},{1,0},{2,3},{3,2},{4,5},{5,4},{6,7},{7,6},{8,9},{9,8},{10,11... | collective-permute-start | bytes 1769480 | tf_op jit(solution)/shard_map/ppermute | solution.py:18
  300.8 10.2 %copy-start.6 = (f32[8,8]{1,0:T(8,128)S(1)}, f32[8,8]{1,0:T(8,128)}, u32[]{:S(2)}) copy-start(f32[8,8]{1,0:T(8,128)} %param.18) | copy-start | bytes 772
  300.8 54.3 %all-to-all-start.2 = ((bf16[32,3,7168]{2,1,0:T(4,128)(2,1)}), bf16[32,3,7168]{2,1,0:T(4,128)(2,1)S(1)}, u32[]{:S(2)}, u32[]{:S(2)}) async-start(bf16[32,3,7168]{2,1,0:T(4,128)(2,1)} %convert_element_type.37), calls=%async_computation.3 | async-start | bytes 3670016 | tf_op jit(solution)/shard_map/all_to_all | solution.py:142
  316.7 4.7 %copy-start.8 = (bf16[8,576]{1,0:T(8,128)(2,1)}, bf16[8,576]{1,0:T(8,128)(2,1)S(1)}, u32[]{:S(2)}) copy-start(bf16[8,576]{1,0:T(8,128)(2,1)S(1)} %get-tuple-element.4) | copy-start | bytes 27652
  316.7 4.7 %copy-start.9 = (bf16[8,576]{1,0:T(8,128)(2,1)}, bf16[8,576]{1,0:T(8,128)(2,1)S(1)}, u32[]{:S(2)}) copy-start(bf16[8,576]{1,0:T(8,128)(2,1)S(1)} %get-tuple-element.5) | copy-start | bytes 27652
  318.8 1.3 copy-start.4
  320.1 1.2 copy-start.2
  320.1 1.2 copy-start.3
  326.7 30.7 %copy-start.5 = (f32[96,8]{0,1:T(8,128)S(1)}, f32[96,8]{0,1:T(8,128)}, u32[]{:S(2)}) copy-start(f32[96,8]{0,1:T(8,128)} %select_reduce_fusion) | copy-start | bytes 9220
Sparse Core Ops, SparseCore 0:
  234.9 61.8 reduce-scatter.1
